TPU v7x, 32 devices: a whole 2x2x4 slice. The times are simulated.
32 devices in a mesh: pipe: 2 (over core), dp: 16 (over z, y, x).
Axes of the slice: x: 2, y: 2, z: 4, core: 2. Of those that a mesh axis runs over, the one named last changes fastest.
Arguments:
- gate: bfloat16 [2, 1, 2048, 4096], P('pipe', None, 'dp'), may hold values from -5 to 5
- filters: bfloat16 [2, 256, 128], P('pipe', 'dp'), may hold values from -0.75 to 0.75
- doc_ids: int32 [1, 2048], P(None, 'dp'), may hold values from 0 to 1, as said below
- loss_grad: bfloat16 [1, 2048, 4096], P(None, 'dp'), may hold values from -6 to 6
Outputs:
- input_grads: bfloat16 [2, 1, 2048, 4096], P('pipe', None, 'dp')
Inputs may be any that keep to these rules, and one draw needn't show every extreme that they name: `doc_ids`: within each window the ids never fall, begin at 0 and end at 1, and every document holds 128 or more tokens.
All inputs are finite; a program needn't handle non-finite values.
Results may differ from a plain program's by a relative error of at most 0.0049.
Values may be sent and summed in bfloat16 or wider, within the bound.
A program may use at most 64 MiB of HBM per device.

v0:
```python
import jax
import jax.numpy as jnp
from jax import lax
from jax.sharding import PartitionSpec as P


def passed_along(value, axis, by):
    count = lax.axis_size(axis)
    pairs = [(i, i + by) for i in range(count) if 0 <= i + by < count]
    return lax.ppermute(value, axis, pairs)


def band_table(filt_block, tap_count):
    groups = filt_block.shape[0]
    span_cols = 2 * tap_count
    base_row = jnp.concatenate(
        [filt_block, jnp.zeros((groups, span_cols + 1 - tap_count), filt_block.dtype)], axis=1
    )
    tiled_rows = jnp.broadcast_to(base_row[:, None, :], (groups, tap_count, span_cols + 1))
    tiled_rows = tiled_rows.reshape(groups, tap_count * (span_cols + 1))
    return tiled_rows[:, : tap_count * span_cols].reshape(groups, tap_count, span_cols)


def adjoint_block(filt_all, scaled_own, scaled_head, parity_own, parity_head):
    row_count, channels = scaled_own.shape
    groups, tap_count = filt_all.shape
    lane_width = channels // groups
    group_block = 64
    block_count = groups // group_block
    row_blocks = row_count // tap_count
    window = jnp.concatenate([scaled_own, scaled_head], axis=0)
    window_parity = jnp.concatenate([parity_own, parity_head], axis=0)
    arranged = window.reshape(
        row_count + tap_count, block_count, group_block, lane_width
    ).transpose(1, 0, 2, 3)
    front_rows = arranged[:, :row_count].reshape(
        block_count, row_blocks, tap_count, group_block, lane_width
    )
    behind = arranged[:, tap_count:].reshape(
        block_count, row_blocks, tap_count, group_block, lane_width
    )
    slabs = jnp.concatenate([front_rows, behind], axis=2)
    column_parity = jnp.concatenate(
        [
            window_parity[:row_count].reshape(row_blocks, tap_count),
            window_parity[tap_count:].reshape(row_blocks, tap_count),
        ],
        axis=1,
    )
    same_doc = parity_own.reshape(row_blocks, tap_count)[:, :, None] == column_parity[:, None, :]
    filt_blocks = filt_all.reshape(block_count, group_block, tap_count)

    def one_block(inputs):
        filt_part, slab_piece = inputs
        band_rows = band_table(filt_part, tap_count)
        masked = jnp.where(same_doc[:, None], band_rows[None], jnp.zeros((), band_rows.dtype))
        return jnp.einsum("rgtj,rjgc->rtgc", masked, slab_piece, preferred_element_type=jnp.float32)

    product = lax.map(one_block, (filt_blocks, slabs))
    return product.transpose(1, 2, 0, 3, 4).reshape(row_count, channels)


def body(gate, filters, doc_ids, loss_grad):
    gate_local = gate[0]
    micro_count, row_count, channels = gate_local.shape
    filt_all = lax.all_gather(filters, "dp", axis=1, tiled=True)[0]
    tap_count = filt_all.shape[1]
    section_count = lax.axis_size("pipe")
    section_index = lax.axis_index("pipe")
    parity = doc_ids % 2
    tick_count = micro_count + section_count - 1
    is_last = section_index == section_count - 1
    is_first = section_index == 0

    def one_tick(tick, carry):
        payload, results = carry
        received = passed_along(payload, "pipe", -1)
        micro_index = tick - (section_count - 1 - section_index)
        active = jnp.logical_and(micro_index >= 0, micro_index < micro_count)
        chosen = jnp.clip(micro_index, 0, micro_count - 1)
        own_loss = lax.dynamic_index_in_dim(loss_grad, chosen, 0, keepdims=False)
        incoming = jnp.where(is_last, own_loss, received)
        gate_now = lax.dynamic_index_in_dim(gate_local, chosen, 0, keepdims=False)
        parity_now = lax.dynamic_index_in_dim(parity, chosen, 0, keepdims=False)
        scaled = (gate_now.astype(jnp.float32) * incoming.astype(jnp.float32)).astype(jnp.bfloat16)
        scaled_head, parity_head = passed_along((scaled, parity_now), "dp", -1)

        def working(unused):
            update = adjoint_block(filt_all, scaled, scaled_head, parity_now, parity_head)
            return (incoming.astype(jnp.float32) + update).astype(jnp.bfloat16)

        def waiting(unused):
            return jnp.zeros_like(incoming)

        produced = lax.cond(active, working, waiting, 0)
        previous = lax.dynamic_index_in_dim(results, chosen, 0, keepdims=False)
        results = lax.dynamic_update_index_in_dim(
            results, jnp.where(active, produced, previous), chosen, 0
        )
        following = jnp.clip(tick + 1, 0, micro_count - 1)
        next_loss = lax.dynamic_index_in_dim(loss_grad, following, 0, keepdims=False)
        payload = jnp.where(is_first, next_loss, produced)
        return (payload, results)

    start_payload = jnp.where(is_first, loss_grad[0], jnp.zeros_like(loss_grad[0]))
    start_results = jnp.zeros_like(gate_local)
    _, results = lax.fori_loop(0, tick_count, one_tick, (start_payload, start_results))
    return results[None]


def solution(mesh):
    return jax.shard_map(
        body,
        mesh=mesh,
        in_specs=(
            P("pipe", None, "dp", None),
            P("pipe", "dp", None),
            P(None, "dp"),
            P(None, "dp", None),
        ),
        out_specs=P("pipe", None, "dp", None),
        check_vma=False,
    )
```

profile of v0, /device:TPU:0, one launch (start us, length us, event | category | flops | bytes accessed | tf_op | source)
XLA Modules:
  0.0 292.6 jit_solution(9645054348732942074)
XLA Ops:
  5.4 43.9 %all_gather.3 = bf16[1,256,128]{2,1,0:T(8,128)(2,1)S(1)} all-gather(bf16[1,16,128]{2,1,0:T(8,128)(2,1)S(1)} %copy-done.1), channel_id=1, replica_groups=mesh['pipe'=2,'dp'=16] {'dp'}, dimensions={1}, use_global_device_ids=true | all-gather | bytes 69632 | tf_op jit(solution)/shard_map/all_gather | solution.py:66
  51.7 238.6 %while.28 = (s32[]{:T(128)}, bf16[128,4096]{0,1:T(8,128)(2,1)}, bf16[1,128,4096]{1,2,0:T(8,128)(2,1)}, pred[]{:T(512)}, bf16[1,128,4096]{1,2,0:T(8,128)(2,1)S(1)...) while((s32[]{:T(128)}, bf16[128,4096]{0,1:T(8,128)(2,1)}, ...), condition=%wide.region_5.6_spmd, body=%wide.region_0.5_spmd.sunk | while | flops 82870536 | bytes 83072224 | solution.py:107
  53.0 3.5 %collective-permute-done = bf16[128,4096]{0,1:T(8,128)(2,1)S(1)} collective-permute-done((bf16[128,4096]{0,1:T(8,128)(2,1)}, bf16[128,4096]{0,1:T(8,128)(2,1)S(1)}, u32[]{:S(2)}, u32[]{:S(2)}) %collective-permute-start) | collective-permute-done | bytes 1048608 | tf_op jit(solution)/shard_map/while/body/eval_jaxpr/ppermute | solution.py:10
  56.5 2.7 fusion.17
  60.4 25.8 %collective-permute-done.1 = bf16[128,4096]{0,1:T(8,128)(2,1)S(1)} collective-permute-done((bf16[128,4096]{0,1:T(8,128)(2,1)S(1)}, bf16[128,4096]{0,1:T(8,128)(2,1)S(1)}, u32[]{:S(2)}, u32[]{:S(2)}) %collective-permute-start.1) | collective-permute-done | bytes 1048608 | tf_op jit(solution)/shard_map/while/body/eval_jaxpr/ppermute | solution.py:10
  86.4 2.7 fusion.18
  90.4 84.5 %collective-permute-done = bf16[128,4096]{0,1:T(8,128)(2,1)S(1)} collective-permute-done((bf16[128,4096]{0,1:T(8,128)(2,1)}, bf16[128,4096]{0,1:T(8,128)(2,1)S(1)}, u32[]{:S(2)}, u32[]{:S(2)}) %collective-permute-start) | collective-permute-done | bytes 1048608 | tf_op jit(solution)/shard_map/while/body/eval_jaxpr/ppermute | solution.py:10
  174.9 2.7 fusion.17
  178.8 25.8 %collective-permute-done.1 = bf16[128,4096]{0,1:T(8,128)(2,1)S(1)} collective-permute-done((bf16[128,4096]{0,1:T(8,128)(2,1)S(1)}, bf16[128,4096]{0,1:T(8,128)(2,1)S(1)}, u32[]{:S(2)}, u32[]{:S(2)}) %collective-permute-start.1) | collective-permute-done | bytes 1048608 | tf_op jit(solution)/shard_map/while/body/eval_jaxpr/ppermute | solution.py:10
  204.6 83.0 %conditional.2 = (bf16[128,4096]{0,1:T(8,128)(2,1)S(1)}) conditional(s32[]{:T(128)} %convert_element_type.55, () %tuple.66, (bf16[128,4096]{0,1:T(8,128)(2,1)}, bf16[1,256,128]{2,1,0:T(8,128)(2,1)S(1)}, bf16[128,4096]{0,1:T(8,128)(2,1)S(1)}, bf16[128,4096]{0,1:T(8,128)(2,1)S(1)}, s32[1,128]{1,0:T(1,128)S(1)}, /*index=5*/s32[128]{0:T(128)S(1)}) %tuple.67), branch_computations={%region_1.1_spmd, %region_2.4_spmd} | conditional | flops 79200512 | bytes 64197568 | solution.py:95
  205.5 80.0 %while.27 = (s32[]{:T(128)}, f32[4,1,128,64,16]{2,4,3,1,0:T(8,128)}, bf16[4,1,256,64,16]{2,4,3,1,0:T(8,128)(2,1)S(1)}, bf16[4,64,128]{2,1,0:T(8,128)(2,1)S(1)}, ...) while((s32[]{:T(128)}, f32[4,1,128,64,16]{2,4,3,1,0:T(8,128)}, ...), condition=%wide.region_4.3_spmd.clone, body=%wide.region_3.2_spmd.clone.sunk | while | flops 69238784 | bytes 47418224 | solution.py:59
  205.6 3.2 %broadcast_in_dim.53 = bf16[64,128,257]{2,1,0:T(8,128)(2,1)} broadcast(bf16[64,257]{1,0:T(8,128)(2,1)S(1)} %concatenate.14), dimensions={0,2} | broadcast | bytes 4243584 | tf_op jit(solution)/shard_map/while/body/eval_jaxpr/cond/branch_1_fun/while/body/eval_jaxpr/broadcast_in_dim | solution.py:19
  208.8 10.8 %reshape.107 = bf16[64,32896]{1,0:T(8,128)(2,1)} reshape(bf16[64,128,257]{2,1,0:T(8,128)(2,1)} %broadcast_in_dim.53) | data formatting | bytes 8421376 | tf_op jit(solution)/shard_map/while/body/eval_jaxpr/cond/branch_1_fun/while/body/eval_jaxpr/reshape | solution.py:20
  219.6 2.2 slice-done
  225.6 3.2 %broadcast_in_dim.53 = bf16[64,128,257]{2,1,0:T(8,128)(2,1)} broadcast(bf16[64,257]{1,0:T(8,128)(2,1)S(1)} %concatenate.14), dimensions={0,2} | broadcast | bytes 4243584 | tf_op jit(solution)/shard_map/while/body/eval_jaxpr/cond/branch_1_fun/while/body/eval_jaxpr/broadcast_in_dim | solution.py:19
  228.8 10.8 %reshape.107 = bf16[64,32896]{1,0:T(8,128)(2,1)} reshape(bf16[64,128,257]{2,1,0:T(8,128)(2,1)} %broadcast_in_dim.53) | data formatting | bytes 8421376 | tf_op jit(solution)/shard_map/while/body/eval_jaxpr/cond/branch_1_fun/while/body/eval_jaxpr/reshape | solution.py:20
  239.6 2.2 slice-done
  245.6 3.2 %broadcast_in_dim.53 = bf16[64,128,257]{2,1,0:T(8,128)(2,1)} broadcast(bf16[64,257]{1,0:T(8,128)(2,1)S(1)} %concatenate.14), dimensions={0,2} | broadcast | bytes 4243584 | tf_op jit(solution)/shard_map/while/body/eval_jaxpr/cond/branch_1_fun/while/body/eval_jaxpr/broadcast_in_dim | solution.py:19
  248.8 10.8 %reshape.107 = bf16[64,32896]{1,0:T(8,128)(2,1)} reshape(bf16[64,128,257]{2,1,0:T(8,128)(2,1)} %broadcast_in_dim.53) | data formatting | bytes 8421376 | tf_op jit(solution)/shard_map/while/body/eval_jaxpr/cond/branch_1_fun/while/body/eval_jaxpr/reshape | solution.py:20
  259.6 2.2 slice-done
  265.6 3.2 %broadcast_in_dim.53 = bf16[64,128,257]{2,1,0:T(8,128)(2,1)} broadcast(bf16[64,257]{1,0:T(8,128)(2,1)S(1)} %concatenate.14), dimensions={0,2} | broadcast | bytes 4243584 | tf_op jit(solution)/shard_map/while/body/eval_jaxpr/cond/branch_1_fun/while/body/eval_jaxpr/broadcast_in_dim | solution.py:19
  268.8 10.8 %reshape.107 = bf16[64,32896]{1,0:T(8,128)(2,1)} reshape(bf16[64,128,257]{2,1,0:T(8,128)(2,1)} %broadcast_in_dim.53) | data formatting | bytes 8421376 | tf_op jit(solution)/shard_map/while/body/eval_jaxpr/cond/branch_1_fun/while/body/eval_jaxpr/reshape | solution.py:20
  287.6 2.7 fusion.18
  290.4 2.3 copy.14
  (53 shorter events, 33.4 us)
Async XLA Ops:
  0.7 49.9 %collective-permute-start.2 = (s32[128]{0:T(128)S(1)}, s32[128]{0:T(128)S(1)}, u32[]{:S(2)}, u32[]{:S(2)}) collective-permute-start(s32[128]{0:T(128)S(1)} %fusion.11), channel_id=1, source_target_pairs={{1,0},{2,1},{3,2},{4,3},{5,4},{6,5},{7,6},{8,7},{9,8},{10,9},{11,1... | collective-permute-start | bytes 1544 | tf_op jit(solution)/shard_map/while/body/eval_jaxpr/ppermute | solution.py:10
  2.6 2.8 copy-start.1
  2.6 46.6 %copy-start = (bf16[1,1,128,4096]{3,2,1,0:T(8,128)(2,1)S(1)}, bf16[1,1,128,4096]{3,2,1,0:T(8,128)(2,1)}, u32[]{:S(2)}) copy-start(bf16[1,1,128,4096]{3,2,1,0:T(8,128)(2,1)} %param.10) | copy-start | bytes 3145732
  51.7 4.8 %collective-permute-start = (bf16[128,4096]{0,1:T(8,128)(2,1)}, bf16[128,4096]{0,1:T(8,128)(2,1)S(1)}, u32[]{:S(2)}, u32[]{:S(2)}) collective-permute-start(bf16[128,4096]{0,1:T(8,128)(2,1)} %get-tuple-element.528), channel_id=1, source_target_pairs={{16,0},{17,1},{18,2},{19,3},{20,4},{21,5},{22,6},{23,7},{24,8},{25... | collective-permute-start | bytes 3145736 | tf_op jit(solution)/shard_map/while/body/eval_jaxpr/ppermute | solution.py:10
  59.1 27.1 %collective-permute-start.1 = (bf16[128,4096]{0,1:T(8,128)(2,1)S(1)}, bf16[128,4096]{0,1:T(8,128)(2,1)S(1)}, u32[]{:S(2)}, u32[]{:S(2)}) collective-permute-start(bf16[128,4096]{0,1:T(8,128)(2,1)S(1)} %get-tuple-element.481), channel_id=1, source_target_pairs={{1,0},{2,1},{3,2},{4,3},{5,4},{6,5},{7,6},{8,7},{9,8},{10,9},{11,1... | collective-permute-start | bytes 3145736 | tf_op jit(solution)/shard_map/while/body/eval_jaxpr/ppermute | solution.py:10
  89.1 85.8 %collective-permute-start = (bf16[128,4096]{0,1:T(8,128)(2,1)}, bf16[128,4096]{0,1:T(8,128)(2,1)S(1)}, u32[]{:S(2)}, u32[]{:S(2)}) collective-permute-start(bf16[128,4096]{0,1:T(8,128)(2,1)} %get-tuple-element.528), channel_id=1, source_target_pairs={{16,0},{17,1},{18,2},{19,3},{20,4},{21,5},{22,6},{23,7},{24,8},{25... | collective-permute-start | bytes 3145736 | tf_op jit(solution)/shard_map/while/body/eval_jaxpr/ppermute | solution.py:10
  177.5 27.1 %collective-permute-start.1 = (bf16[128,4096]{0,1:T(8,128)(2,1)S(1)}, bf16[128,4096]{0,1:T(8,128)(2,1)S(1)}, u32[]{:S(2)}, u32[]{:S(2)}) collective-permute-start(bf16[128,4096]{0,1:T(8,128)(2,1)S(1)} %get-tuple-element.481), channel_id=1, source_target_pairs={{1,0},{2,1},{3,2},{4,3},{5,4},{6,5},{7,6},{8,7},{9,8},{10,9},{11,1... | collective-permute-start | bytes 3145736 | tf_op jit(solution)/shard_map/while/body/eval_jaxpr/ppermute | solution.py:10
  219.6 2.2 slice-start
  239.6 2.2 slice-start
  259.6 2.2 slice-start
  279.6 2.2 slice-start
where the time goes:
time: 294 us; the launch traced here: 293 us
  waiting for transfers between devices  140 us (48%)
  local copies, waits for them, and re-layouts  76.3 us (26%)
  blocking collectives  43.9 us (15%)
  other arithmetic  18.2 us (6%)
  matrix products  8.04 us (3%)
  starting transfers between devices  6.4 us (2%)
    ppermute x5, waiting for transfers between devices, passed_along(): return lax.ppermute(value, axis, pairs)  140 us
    all_gather x1, blocking collectives, body(): filt_all = lax.all_gather(filters, 'dp', axis=1, tiled=True)[0]  43.9 us
    reshape x4, local copies, waits for them, and re-layouts, band_table(): tiled_rows = tiled_rows.reshape(groups, tap_count * (span_cols + 1))  43.4 us
    broadcast_in_dim x4, local copies, waits for them, and re-layouts, band_table(): jnp.broadcast_to(base_row[:, None, :], (groups, tap_count, span_cols + 1))  12.8 us
    slice x8, local copies, waits for them, and re-layouts, band_table(): tiled_rows[:, :tap_count * span_cols].reshape(groups, tap_count, span_cols)  8.75 us
    dot_general x4, matrix products, one_block(): jnp.einsum('rgtj,rjgc->rtgc', masked, slab_piece, preferred_element_type=...  8.04 us
    ppermute x5, starting transfers between devices, passed_along(): return lax.ppermute(value, axis, pairs)  6.4 us
  transfers between devices with their start and end apart: 5, of which 4 were waited for; matrix products, arithmetic and copies ran while one was open for 2% of the time, Pallas kernels for 0%

commit v1 on v0

--- a/solution.py
+++ b/solution.py
@@ -2,6 +2,27 @@
 import jax.numpy as jnp
 from jax import lax
 from jax.sharding import PartitionSpec as P
+
+
+def in_order(pieces, dim):
+    pieces = jnp.moveaxis(pieces, 0, dim)
+    dims = pieces.shape
+    return pieces.reshape(*dims[:dim], dims[dim] * dims[dim + 1], *dims[dim + 2 :])
+
+
+def doubled(value, axis):
+    size, mine = (lax.axis_size(axis), lax.axis_index(axis))
+    parts, bit = (value[None], 1)
+    while bit < size:
+        theirs = lax.ppermute(parts, axis, [(i, i ^ bit) for i in range(size)])
+        low = mine & bit == 0
+        parts = jnp.concatenate([jnp.where(low, parts, theirs), jnp.where(low, theirs, parts)])
+        bit *= 2
+    return parts
+
+
+def collect(array, axis, dim):
+    return in_order(doubled(array, axis), dim)
 
 
 def passed_along(value, axis, by):
@@ -63,7 +84,7 @@
 def body(gate, filters, doc_ids, loss_grad):
     gate_local = gate[0]
     micro_count, row_count, channels = gate_local.shape
-    filt_all = lax.all_gather(filters, "dp", axis=1, tiled=True)[0]
+    filt_all = collect(filters, "dp", 1)[0]
     tap_count = filt_all.shape[1]
     section_count = lax.axis_size("pipe")
     section_index = lax.axis_index("pipe")

time: 294 us -> 266 us (0.905)
  blocking collectives: 43.9 us -> 0 us
  starting transfers between devices: 6.4 us -> 18.1 us
  waiting for transfers between devices: 140 us -> 143 us
    all_gather x1 -> x0, blocking collectives: 43.9 us -> none  [body(): filt_all = lax.all_gather(filters, 'dp', axis=1, tiled=True)[0]]
    ppermute x0 -> x4, starting transfers between devices: none -> 11.7 us  [doubled(): theirs = lax.ppermute(parts, axis, [(i, i ^ bit) for i in range(size)])]
    ppermute x0 -> x4, waiting for transfers between devices: none -> 3.01 us  [doubled(): theirs = lax.ppermute(parts, axis, [(i, i ^ bit) for i in range(size)])]
  transfers between devices with their start and end apart: 5 -> 9, of which waited for: 4 -> 7; matrix products, arithmetic and copies ran while one was open for 2% -> 2% of each run, Pallas kernels for 0% -> 0%
where the time goes in v1:
time: 266 us; the launch traced here: 264 us
  waiting for transfers between devices  143 us (54%)
  local copies, waits for them, and re-layouts  76.5 us (29%)
  other arithmetic  18.3 us (7%)
  starting transfers between devices  18.1 us (7%)
  matrix products  8.09 us (3%)
    ppermute x5, waiting for transfers between devices, passed_along(): return lax.ppermute(value, axis, pairs)  140 us
    reshape x4, local copies, waits for them, and re-layouts, band_table(): tiled_rows = tiled_rows.reshape(groups, tap_count * (span_cols + 1))  43.5 us
    broadcast_in_dim x4, local copies, waits for them, and re-layouts, band_table(): jnp.broadcast_to(base_row[:, None, :], (groups, tap_count, span_cols + 1))  12.8 us
    ppermute x4, starting transfers between devices, doubled(): theirs = lax.ppermute(parts, axis, [(i, i ^ bit) for i in range(size)])  11.7 us
    slice x8, local copies, waits for them, and re-layouts, band_table(): tiled_rows[:, :tap_count * span_cols].reshape(groups, tap_count, span_cols)  8.75 us
    dot_general x4, matrix products, one_block(): jnp.einsum('rgtj,rjgc->rtgc', masked, slab_piece, preferred_element_type=...  8.09 us
    ppermute x5, starting transfers between devices, passed_along(): return lax.ppermute(value, axis, pairs)  6.4 us
    broadcast_in_dim x2, other arithmetic, one_tick(): lax.dynamic_update_index_in_dim(results, jnp.where(active, produced, prev...  5.43 us
  transfers between devices with their start and end apart: 9, of which 7 were waited for; matrix products, arithmetic and copies ran while one was open for 2% of the time, Pallas kernels for 0%

profile of v1, /device:TPU:0, one launch (start us, length us, event | category | flops | bytes accessed | tf_op | source)
XLA Modules:
  0.0 264.3 jit_solution(3437398901802618344)
XLA Ops:
  0.0 2.9 %collective-permute-start.2 = (bf16[1,1,16,128]{3,2,0,1:T(8,128)(2,1)}, bf16[1,1,16,128]{3,2,0,1:T(8,128)(2,1)S(1)}, u32[]{:S(2)}, u32[]{:S(2)}) collective-permute-start(bf16[1,1,16,128]{3,2,0,1:T(8,128)(2,1)} %bitcast.86), channel_id=1, source_target_pairs={{0,1},{1,0},{2,3},{3,2},{4,5},{5,4},{6,7},{7,6},{8,9},{9,8},{10,11... | collective-permute-start | bytes 12296 | tf_op jit(solution)/shard_map/ppermute | solution.py:17
  11.2 3.6 %collective-permute-start.4 = (bf16[4,1,16,128]{3,2,0,1:T(8,128)(2,1)S(1)}, bf16[4,1,16,128]{3,2,0,1:T(8,128)(2,1)S(1)}, u32[]{:S(2)}, u32[]{:S(2)}) collective-permute-start(bf16[4,1,16,128]{3,2,0,1:T(8,128)(2,1)S(1)} %pad_maximum_fusion.4), channel_id=1, source_target_pairs={{0,4},{1,5},{2,6},{3,7},{4,0},{5,1},{6,2},{7,3},{8,12},{9,13},{10,... | collective-permute-start | bytes 49160 | tf_op jit(solution)/shard_map/ppermute | solution.py:17
  16.5 3.2 %collective-permute-start.5 = (bf16[8,1,16,128]{3,2,0,1:T(8,128)(2,1)S(1)}, bf16[8,1,16,128]{3,2,0,1:T(8,128)(2,1)S(1)}, u32[]{:S(2)}, u32[]{:S(2)}) collective-permute-start(bf16[8,1,16,128]{3,2,0,1:T(8,128)(2,1)S(1)} %pad_maximum_fusion.3), channel_id=1, source_target_pairs={{0,8},{1,9},{2,10},{3,11},{4,12},{5,13},{6,14},{7,15},{8,0},{9,1},... | collective-permute-start | bytes 98312 | tf_op jit(solution)/shard_map/ppermute | solution.py:17
  22.8 239.3 %while.28 = (s32[]{:T(128)}, bf16[128,4096]{0,1:T(8,128)(2,1)}, bf16[1,128,4096]{1,2,0:T(8,128)(2,1)}, pred[]{:T(512)}, bf16[1,128,4096]{1,2,0:T(8,128)(2,1)S(1)...) while((s32[]{:T(128)}, bf16[128,4096]{0,1:T(8,128)(2,1)}, ...), condition=%wide.region_5.6_spmd, body=%wide.region_0.5_spmd.sunk | while | flops 82870536 | bytes 83072224 | solution.py:128
  24.0 3.5 %collective-permute-done = bf16[128,4096]{0,1:T(8,128)(2,1)S(1)} collective-permute-done((bf16[128,4096]{0,1:T(8,128)(2,1)}, bf16[128,4096]{0,1:T(8,128)(2,1)S(1)}, u32[]{:S(2)}, u32[]{:S(2)}) %collective-permute-start) | collective-permute-done | bytes 1048608 | tf_op jit(solution)/shard_map/while/body/eval_jaxpr/ppermute | solution.py:31
  27.5 2.7 %fusion.17 = (bf16[128,4096]{0,1:T(8,128)(2,1)S(1)}, bf16[128,4096]{0,1:T(8,128)(2,1)}) fusion(bf16[1,128,4096]{1,2,0:T(8,128)(2,1)} %get-tuple-element.554, bf16[128,4096]{0,1:T(8,128)(2,1)S(1)} %collective-permute-done, bf16[1,128,4096]{1,2,0:T(8,128)(2,1)S(1)} %get-tuple-element.552, pred[]{:T(512)} %get-tuple-element.555), kind=kLoop, calls=%fused_computation.17.clone.1 | loop fusion | flops 2621440 | bytes 5242881 | tf_op jit(solution)/shard_map/while/body/eval_jaxpr/convert_element_type | solution.py:106
  31.5 25.8 %collective-permute-done.1 = bf16[128,4096]{0,1:T(8,128)(2,1)S(1)} collective-permute-done((bf16[128,4096]{0,1:T(8,128)(2,1)S(1)}, bf16[128,4096]{0,1:T(8,128)(2,1)S(1)}, u32[]{:S(2)}, u32[]{:S(2)}) %collective-permute-start.1) | collective-permute-done | bytes 1048608 | tf_op jit(solution)/shard_map/while/body/eval_jaxpr/ppermute | solution.py:31
  57.4 2.7 %fusion.18 = (bf16[1,128,4096]{1,2,0:T(8,128)(2,1)}, bf16[128,4096]{0,1:T(8,128)(2,1)}) fusion(bf16[128,4096]{0,1:T(8,128)(2,1)S(1)} %get-tuple-element.561, bf16[1,128,4096]{1,2,0:T(8,128)(2,1)} %get-tuple-element.537, pred[]{:T(512)S(6)} %and.37, bf16[1,128,4096]{1,2,0:T(8,128)(2,1)S(1)} %get-tuple-element.552, pred[]{:T(512)} %get-tuple-element.551), kind=kLoop, calls=%fused_computation.19.clone.1 | loop fusion | flops 1048576 | bytes 5242882 | tf_op jit(solution)/shard_map/while/body/eval_jaxpr/jit(dynamic_update_index_in_dim)/broadcast_in_dim | solution.py:118
  61.4 84.8 %collective-permute-done = bf16[128,4096]{0,1:T(8,128)(2,1)S(1)} collective-permute-done((bf16[128,4096]{0,1:T(8,128)(2,1)}, bf16[128,4096]{0,1:T(8,128)(2,1)S(1)}, u32[]{:S(2)}, u32[]{:S(2)}) %collective-permute-start) | collective-permute-done | bytes 1048608 | tf_op jit(solution)/shard_map/while/body/eval_jaxpr/ppermute | solution.py:31
  146.2 2.7 %fusion.17 = (bf16[128,4096]{0,1:T(8,128)(2,1)S(1)}, bf16[128,4096]{0,1:T(8,128)(2,1)}) fusion(bf16[1,128,4096]{1,2,0:T(8,128)(2,1)} %get-tuple-element.554, bf16[128,4096]{0,1:T(8,128)(2,1)S(1)} %collective-permute-done, bf16[1,128,4096]{1,2,0:T(8,128)(2,1)S(1)} %get-tuple-element.552, pred[]{:T(512)} %get-tuple-element.555), kind=kLoop, calls=%fused_computation.17.clone.1 | loop fusion | flops 2621440 | bytes 5242881 | tf_op jit(solution)/shard_map/while/body/eval_jaxpr/convert_element_type | solution.py:106
  150.1 25.9 %collective-permute-done.1 = bf16[128,4096]{0,1:T(8,128)(2,1)S(1)} collective-permute-done((bf16[128,4096]{0,1:T(8,128)(2,1)S(1)}, bf16[128,4096]{0,1:T(8,128)(2,1)S(1)}, u32[]{:S(2)}, u32[]{:S(2)}) %collective-permute-start.1) | collective-permute-done | bytes 1048608 | tf_op jit(solution)/shard_map/while/body/eval_jaxpr/ppermute | solution.py:31
  176.1 83.2 %conditional.2 = (bf16[128,4096]{0,1:T(8,128)(2,1)S(1)}) conditional(s32[]{:T(128)} %convert_element_type.55, () %tuple.70, (bf16[128,4096]{0,1:T(8,128)(2,1)}, bf16[16,1,16,128]{3,2,0,1:T(8,128)(2,1)S(1)}, bf16[128,4096]{0,1:T(8,128)(2,1)S(1)}, bf16[128,4096]{0,1:T(8,128)(2,1)S(1)}, s32[1,128]{1,0:T(1,128)S(1)}, /*index=5*/s32[128]{0:T(128)S(1)}) %tuple.71), branch_computations={%region_1.1_spmd, %region_2.4_spmd} | conditional | flops 79200512 | bytes 64197568 | solution.py:116
  177.0 80.3 %while.27 = (s32[]{:T(128)}, f32[4,1,128,64,16]{2,4,3,1,0:T(8,128)}, bf16[4,1,256,64,16]{2,4,3,1,0:T(8,128)(2,1)S(1)}, bf16[4,64,128]{2,1,0:T(8,128)(2,1)S(1)}, ...) while((s32[]{:T(128)}, f32[4,1,128,64,16]{2,4,3,1,0:T(8,128)}, ...), condition=%wide.region_4.3_spmd.clone, body=%wide.region_3.2_spmd.clone.sunk | while | flops 69238784 | bytes 47418224 | solution.py:80
  177.0 3.2 %broadcast_in_dim.57 = bf16[64,128,257]{2,1,0:T(8,128)(2,1)} broadcast(bf16[64,257]{1,0:T(8,128)(2,1)S(1)} %concatenate.30), dimensions={0,2} | broadcast | bytes 4243584 | tf_op jit(solution)/shard_map/while/body/eval_jaxpr/cond/branch_1_fun/while/body/eval_jaxpr/broadcast_in_dim | solution.py:40
  180.2 10.9 %reshape.107 = bf16[64,32896]{1,0:T(8,128)(2,1)} reshape(bf16[64,128,257]{2,1,0:T(8,128)(2,1)} %broadcast_in_dim.57) | data formatting | bytes 8421376 | tf_op jit(solution)/shard_map/while/body/eval_jaxpr/cond/branch_1_fun/while/body/eval_jaxpr/reshape | solution.py:41
  191.1 2.2 slice-done
  197.1 3.2 %broadcast_in_dim.57 = bf16[64,128,257]{2,1,0:T(8,128)(2,1)} broadcast(bf16[64,257]{1,0:T(8,128)(2,1)S(1)} %concatenate.30), dimensions={0,2} | broadcast | bytes 4243584 | tf_op jit(solution)/shard_map/while/body/eval_jaxpr/cond/branch_1_fun/while/body/eval_jaxpr/broadcast_in_dim | solution.py:40
  200.3 10.9 %reshape.107 = bf16[64,32896]{1,0:T(8,128)(2,1)} reshape(bf16[64,128,257]{2,1,0:T(8,128)(2,1)} %broadcast_in_dim.57) | data formatting | bytes 8421376 | tf_op jit(solution)/shard_map/while/body/eval_jaxpr/cond/branch_1_fun/while/body/eval_jaxpr/reshape | solution.py:41
  217.1 3.2 %broadcast_in_dim.57 = bf16[64,128,257]{2,1,0:T(8,128)(2,1)} broadcast(bf16[64,257]{1,0:T(8,128)(2,1)S(1)} %concatenate.30), dimensions={0,2} | broadcast | bytes 4243584 | tf_op jit(solution)/shard_map/while/body/eval_jaxpr/cond/branch_1_fun/while/body/eval_jaxpr/broadcast_in_dim | solution.py:40
  220.3 10.9 %reshape.107 = bf16[64,32896]{1,0:T(8,128)(2,1)} reshape(bf16[64,128,257]{2,1,0:T(8,128)(2,1)} %broadcast_in_dim.57) | data formatting | bytes 8421376 | tf_op jit(solution)/shard_map/while/body/eval_jaxpr/cond/branch_1_fun/while/body/eval_jaxpr/reshape | solution.py:41
  237.2 3.2 %broadcast_in_dim.57 = bf16[64,128,257]{2,1,0:T(8,128)(2,1)} broadcast(bf16[64,257]{1,0:T(8,128)(2,1)S(1)} %concatenate.30), dimensions={0,2} | broadcast | bytes 4243584 | tf_op jit(solution)/shard_map/while/body/eval_jaxpr/cond/branch_1_fun/while/body/eval_jaxpr/broadcast_in_dim | solution.py:40
  240.4 10.9 %reshape.107 = bf16[64,32896]{1,0:T(8,128)(2,1)} reshape(bf16[64,128,257]{2,1,0:T(8,128)(2,1)} %broadcast_in_dim.57) | data formatting | bytes 8421376 | tf_op jit(solution)/shard_map/while/body/eval_jaxpr/cond/branch_1_fun/while/body/eval_jaxpr/reshape | solution.py:41
  259.3 2.7 %fusion.18 = (bf16[1,128,4096]{1,2,0:T(8,128)(2,1)}, bf16[128,4096]{0,1:T(8,128)(2,1)}) fusion(bf16[128,4096]{0,1:T(8,128)(2,1)S(1)} %get-tuple-element.561, bf16[1,128,4096]{1,2,0:T(8,128)(2,1)} %get-tuple-element.537, pred[]{:T(512)S(6)} %and.37, bf16[1,128,4096]{1,2,0:T(8,128)(2,1)S(1)} %get-tuple-element.552, pred[]{:T(512)} %get-tuple-element.551), kind=kLoop, calls=%fused_computation.19.clone.1 | loop fusion | flops 1048576 | bytes 5242882 | tf_op jit(solution)/shard_map/while/body/eval_jaxpr/jit(dynamic_update_index_in_dim)/broadcast_in_dim | solution.py:118
  262.0 2.3 copy.14
  (68 shorter events, 42.9 us)
Async XLA Ops:
  0.0 4.7 %collective-permute-start.2 = (bf16[1,1,16,128]{3,2,0,1:T(8,128)(2,1)}, bf16[1,1,16,128]{3,2,0,1:T(8,128)(2,1)S(1)}, u32[]{:S(2)}, u32[]{:S(2)}) collective-permute-start(bf16[1,1,16,128]{3,2,0,1:T(8,128)(2,1)} %bitcast.86), channel_id=1, source_target_pairs={{0,1},{1,0},{2,3},{3,2},{4,5},{5,4},{6,7},{7,6},{8,9},{9,8},{10,11... | collective-permute-start | bytes 12296 | tf_op jit(solution)/shard_map/ppermute | solution.py:17
  5.4 5.8 %collective-permute-start.3 = (bf16[2,1,16,128]{3,2,0,1:T(8,128)(2,1)S(1)}, bf16[2,1,16,128]{3,2,0,1:T(8,128)(2,1)S(1)}, u32[]{:S(2)}, u32[]{:S(2)}) collective-permute-start(bf16[2,1,16,128]{3,2,0,1:T(8,128)(2,1)S(1)} %pad_maximum_fusion.5), channel_id=1, source_target_pairs={{0,2},{1,3},{2,0},{3,1},{4,6},{5,7},{6,4},{7,5},{8,10},{9,11},{10,... | collective-permute-start | bytes 24584 | tf_op jit(solution)/shard_map/ppermute | solution.py:17
  8.1 13.5 %collective-permute-start.6 = (s32[128]{0:T(128)S(1)}, s32[128]{0:T(128)S(1)}, u32[]{:S(2)}, u32[]{:S(2)}) collective-permute-start(s32[128]{0:T(128)S(1)} %fusion.11), channel_id=1, source_target_pairs={{1,0},{2,1},{3,2},{4,3},{5,4},{6,5},{7,6},{8,7},{9,8},{10,9},{11,1... | collective-permute-start | bytes 1544 | tf_op jit(solution)/shard_map/while/body/eval_jaxpr/ppermute | solution.py:31
  9.4 10.3 %copy-start.1 = (s32[1,128]{1,0:T(1,128)S(1)}, s32[1,128]{1,0:T(1,128)}, u32[]{:S(2)}) copy-start(s32[1,128]{1,0:T(1,128)} %param.12) | copy-start | bytes 1540
  9.5 10.3 %copy-start = (bf16[1,1,128,4096]{3,2,1,0:T(8,128)(2,1)S(1)}, bf16[1,1,128,4096]{3,2,1,0:T(8,128)(2,1)}, u32[]{:S(2)}) copy-start(bf16[1,1,128,4096]{3,2,1,0:T(8,128)(2,1)} %param.10) | copy-start | bytes 3145732
  11.2 5.3 %collective-permute-start.4 = (bf16[4,1,16,128]{3,2,0,1:T(8,128)(2,1)S(1)}, bf16[4,1,16,128]{3,2,0,1:T(8,128)(2,1)S(1)}, u32[]{:S(2)}, u32[]{:S(2)}) collective-permute-start(bf16[4,1,16,128]{3,2,0,1:T(8,128)(2,1)S(1)} %pad_maximum_fusion.4), channel_id=1, source_target_pairs={{0,4},{1,5},{2,6},{3,7},{4,0},{5,1},{6,2},{7,3},{8,12},{9,13},{10,... | collective-permute-start | bytes 49160 | tf_op jit(solution)/shard_map/ppermute | solution.py:17
  16.5 5.1 %collective-permute-start.5 = (bf16[8,1,16,128]{3,2,0,1:T(8,128)(2,1)S(1)}, bf16[8,1,16,128]{3,2,0,1:T(8,128)(2,1)S(1)}, u32[]{:S(2)}, u32[]{:S(2)}) collective-permute-start(bf16[8,1,16,128]{3,2,0,1:T(8,128)(2,1)S(1)} %pad_maximum_fusion.3), channel_id=1, source_target_pairs={{0,8},{1,9},{2,10},{3,11},{4,12},{5,13},{6,14},{7,15},{8,0},{9,1},... | collective-permute-start | bytes 98312 | tf_op jit(solution)/shard_map/ppermute | solution.py:17
  22.8 4.8 %collective-permute-start = (bf16[128,4096]{0,1:T(8,128)(2,1)}, bf16[128,4096]{0,1:T(8,128)(2,1)S(1)}, u32[]{:S(2)}, u32[]{:S(2)}) collective-permute-start(bf16[128,4096]{0,1:T(8,128)(2,1)} %get-tuple-element.536), channel_id=1, source_target_pairs={{16,0},{17,1},{18,2},{19,3},{20,4},{21,5},{22,6},{23,7},{24,8},{25... | collective-permute-start | bytes 3145736 | tf_op jit(solution)/shard_map/while/body/eval_jaxpr/ppermute | solution.py:31
  30.2 27.1 %collective-permute-start.1 = (bf16[128,4096]{0,1:T(8,128)(2,1)S(1)}, bf16[128,4096]{0,1:T(8,128)(2,1)S(1)}, u32[]{:S(2)}, u32[]{:S(2)}) collective-permute-start(bf16[128,4096]{0,1:T(8,128)(2,1)S(1)} %get-tuple-element.489), channel_id=1, source_target_pairs={{1,0},{2,1},{3,2},{4,3},{5,4},{6,5},{7,6},{8,7},{9,8},{10,9},{11,1... | collective-permute-start | bytes 3145736 | tf_op jit(solution)/shard_map/while/body/eval_jaxpr/ppermute | solution.py:31
  60.1 86.0 %collective-permute-start = (bf16[128,4096]{0,1:T(8,128)(2,1)}, bf16[128,4096]{0,1:T(8,128)(2,1)S(1)}, u32[]{:S(2)}, u32[]{:S(2)}) collective-permute-start(bf16[128,4096]{0,1:T(8,128)(2,1)} %get-tuple-element.536), channel_id=1, source_target_pairs={{16,0},{17,1},{18,2},{19,3},{20,4},{21,5},{22,6},{23,7},{24,8},{25... | collective-permute-start | bytes 3145736 | tf_op jit(solution)/shard_map/while/body/eval_jaxpr/ppermute | solution.py:31
  148.8 27.2 %collective-permute-start.1 = (bf16[128,4096]{0,1:T(8,128)(2,1)S(1)}, bf16[128,4096]{0,1:T(8,128)(2,1)S(1)}, u32[]{:S(2)}, u32[]{:S(2)}) collective-permute-start(bf16[128,4096]{0,1:T(8,128)(2,1)S(1)} %get-tuple-element.489), channel_id=1, source_target_pairs={{1,0},{2,1},{3,2},{4,3},{5,4},{6,5},{7,6},{8,7},{9,8},{10,9},{11,1... | collective-permute-start | bytes 3145736 | tf_op jit(solution)/shard_map/while/body/eval_jaxpr/ppermute | solution.py:31
  191.1 2.2 slice-start
  211.2 2.2 slice-start
  231.2 2.2 slice-start
  251.3 2.2 slice-start
